TPU v7x, 256 devices: a whole 4x4x8 slice. The times are simulated.
256 devices in a mesh: seq: 16 (over x_lo, y, core), head: 16 (over x_hi, z).
Axes of the slice: x: 4 (x_hi: 2, x_lo: 2; x = x_hi * 2 + x_lo), y: 4, z: 8, core: 2. Of those that a mesh axis runs over, the one named last changes fastest.
Arguments:
- query_heads: bfloat16 [16, 16384, 128], P('head', 'seq'), may hold values from -6 to 6
- key_heads: bfloat16 [2, 16384, 128], P(None, ('seq', 'head')), may hold values from -6 to 6
- value_heads: bfloat16 [2, 16384, 128], P(None, ('seq', 'head')), may hold values from -6 to 6
- doc_lengths: int32 [16], replicated, may hold values from 1 to 8192, 16384 in all
Outputs:
- attended: bfloat16 [16, 16384, 128], P('head', 'seq')
Inputs may be any that keep to these rules, and one draw needn't show every extreme that they name: `doc_lengths`: the lengths sum to 16384; documents lie end to end in order.
All inputs are finite; a program needn't handle non-finite values.
Results may differ from a plain program's by a relative error of at most 0.0049.
Values may be sent and summed in bfloat16 or wider, within the bound.
A program may use at most 64 MiB of HBM per device.

v0:
```python
import math

import jax
import jax.numpy as jnp
from jax import lax
from jax.sharding import PartitionSpec as P

QH = 16
KVH = 2


NEG = -1e30
NO_LIMIT = 1 << 30


def doc_first(doc_lengths, positions):
    doc_ends = jnp.cumsum(doc_lengths)
    starts = doc_ends - doc_lengths
    inside = starts[None, :] <= positions[:, None]
    return jnp.max(jnp.where(inside, starts[None, :], 0), axis=1)


def attend(
    query_rows,
    query_pos,
    query_first,
    key_rows,
    value_rows,
    key_pos,
    low_limit,
    high_limit,
    weighted,
    running,
    totals,
):
    score_scale = 1.0 / math.sqrt(query_rows.shape[-1])
    scores = (
        jnp.einsum("rd,kd->rk", query_rows, key_rows, preferred_element_type=jnp.float32)
        * score_scale
    )
    key_line = key_pos[None, :]
    visible = (key_line <= query_pos[:, None]) & (key_line >= query_first[:, None])
    visible = visible & (key_line >= low_limit) & (key_line <= high_limit)
    new_peak = jnp.maximum(running, jnp.max(jnp.where(visible, scores, NEG), axis=1))
    weights = jnp.where(visible, jnp.exp(scores - new_peak[:, None]), 0.0)
    factor = jnp.exp(running - new_peak)
    weighted = weighted * factor[:, None] + jnp.dot(
        weights.astype(jnp.bfloat16), value_rows, preferred_element_type=jnp.float32
    )
    totals = totals * factor + jnp.sum(weights, axis=1)
    return (weighted, new_peak, totals)


def update_state(one_state, one_spec, key_rows, value_rows, key_start):
    query_blocks, pos_blocks, first_blocks, low_limit, high_limit = one_spec
    key_count = key_rows.shape[0]
    key_pos = key_start + jnp.arange(key_count, dtype=jnp.int32)
    key_last = key_start + key_count - 1

    def per_block(packed):
        query_rows, query_pos, query_first, weighted, running, totals = packed
        useful = (key_start <= jnp.max(query_pos)) & (key_last >= jnp.min(query_first))
        useful = useful & (key_last >= low_limit) & (key_start <= high_limit)

        def compute(current):
            return attend(
                query_rows,
                query_pos,
                query_first,
                key_rows,
                value_rows,
                key_pos,
                low_limit,
                high_limit,
                current[0],
                current[1],
                current[2],
            )

        return lax.cond(useful, compute, lambda current: current, (weighted, running, totals))

    return lax.map(per_block, (query_blocks, pos_blocks, first_blocks) + tuple(one_state))


def make_fold(row_specs):

    def fold_keys(states, pieces, piece_start):
        key_piece, value_piece = pieces
        piece_rows = key_piece.shape[0]
        step_rows = math.gcd(512, piece_rows)

        def one_step(step_index, current):
            offset = step_index * step_rows
            key_rows = lax.dynamic_slice_in_dim(key_piece, offset, step_rows, 0)
            value_rows = lax.dynamic_slice_in_dim(value_piece, offset, step_rows, 0)
            return tuple(
                (
                    update_state(one_state, one_spec, key_rows, value_rows, offset)
                    for one_state, one_spec in zip(current, row_specs)
                )
            )

        return lax.fori_loop(0, piece_rows // step_rows, one_step, states)

    return fold_keys


def row_spec(local_heads, positions, doc_lengths, low_limit, high_limit):
    heads_here, tok_rows, width = local_heads.shape
    total_rows = heads_here * tok_rows
    block_rows = math.gcd(512, total_rows)
    block_count = total_rows // block_rows
    query_blocks = local_heads.reshape(block_count, block_rows, width)
    row_pos = jnp.tile(positions, heads_here)
    row_first = doc_first(doc_lengths, row_pos)
    return (
        query_blocks,
        row_pos.reshape(block_count, block_rows),
        row_first.reshape(block_count, block_rows),
        low_limit,
        high_limit,
    )


def empty_state(one_spec):
    query_blocks = one_spec[0]
    block_count, block_rows, width = query_blocks.shape
    return (
        jnp.zeros((block_count, block_rows, width), jnp.float32),
        jnp.full((block_count, block_rows), NEG, jnp.float32),
        jnp.zeros((block_count, block_rows), jnp.float32),
    )


def local(query_heads, key_heads, value_heads, doc_lengths):
    cycle_index = lax.axis_index("seq")
    heads_here, tok_rows, width = query_heads.shape
    head_group = lax.axis_index("head") * heads_here // (QH // KVH)
    own_positions = cycle_index * tok_rows + jnp.arange(tok_rows, dtype=jnp.int32)
    row_specs = (row_spec(query_heads, own_positions, doc_lengths, 0, NO_LIMIT),)
    initial = tuple((empty_state(one_spec) for one_spec in row_specs))
    gathered_keys, gathered_values = (
        lax.all_gather(key_heads, "head", axis=1, tiled=True),
        lax.all_gather(value_heads, "head", axis=1, tiled=True),
    )
    group_keys = lax.dynamic_index_in_dim(gathered_keys, head_group, 0, keepdims=False)
    group_values = lax.dynamic_index_in_dim(gathered_values, head_group, 0, keepdims=False)
    fold_keys = make_fold(row_specs)
    states = fold_keys(
        initial,
        (
            lax.all_gather(group_keys, "seq", axis=0, tiled=True),
            lax.all_gather(group_values, "seq", axis=0, tiled=True),
        ),
        jnp.int32(0),
    )
    weighted, running, totals = states[0]
    attended = (weighted / totals[:, :, None]).astype(jnp.bfloat16)
    return attended.reshape(heads_here, tok_rows, width)


def solution(mesh):
    placed = (
        P("head", "seq", None),
        P(None, ("seq", "head"), None),
        P(None, ("seq", "head"), None),
        P(),
    )
    return jax.shard_map(
        local, mesh=mesh, in_specs=placed, out_specs=P("head", "seq", None), check_vma=False
    )
```

profile of v0, /device:TPU:27, one launch (start us, length us, event | category | flops | bytes accessed | tf_op | source)
XLA Modules:
  0.0 612.3 jit_solution(3927813570713768917)
XLA Ops:
  6.5 39.0 %all_gather.14 = bf16[2,1024,128]{2,1,0:T(8,128)(2,1)S(1)} all-gather(bf16[2,64,128]{2,1,0:T(8,128)(2,1)} %param.12), channel_id=1, replica_groups=mesh['seq'=16,'head'=16] {'head'}, dimensions={1}, use_global_device_ids=true | all-gather | bytes 557056 | tf_op jit(solution)/shard_map/all_gather | solution.py:144
  46.3 32.4 %all_gather.12 = bf16[2,1024,128]{2,1,0:T(8,128)(2,1)S(1)} all-gather(bf16[2,64,128]{2,1,0:T(8,128)(2,1)} %param.11), channel_id=1, replica_groups=mesh['seq'=16,'head'=16] {'head'}, dimensions={1}, use_global_device_ids=true | all-gather | bytes 557056 | tf_op jit(solution)/shard_map/all_gather | solution.py:143
  81.1 7.3 %all-gather.7.cloned.1.call-done = bf16[1,16384,128]{2,1,0:T(8,128)(2,1)} async-done(((bf16[1,1024,128]{2,1,0:T(8,128)(2,1)}), bf16[1,16384,128]{2,1,0:T(8,128)(2,1)}) %all-gather.7.cloned.1.call-update) | async-done | bytes 4194320 | tf_op jit(solution)/shard_map/all_gather | solution.py:153
  88.4 41.1 %all-gather.5.cloned.1.call-done = bf16[1,16384,128]{2,1,0:T(8,128)(2,1)} async-done(((bf16[1,1024,128]{2,1,0:T(8,128)(2,1)}), bf16[1,16384,128]{2,1,0:T(8,128)(2,1)}) %all-gather.5.cloned.1.call-update) | async-done | bytes 4194320 | tf_op jit(solution)/shard_map/all_gather | solution.py:152
  129.6 474.9 %while.63 = (s32[]{:T(128)}, f32[2,512,128]{2,1,0:T(8,128)S(1)}, f32[2,512]{1,0:T(2,128)S(1)}, f32[2,512]{1,0:T(2,128)S(1)}, bf16[16384,128]{1,0:T(8,128)(2,1)},...) while((s32[]{:T(128)}, f32[2,512,128]{2,1,0:T(8,128)S(1)}, ...), condition=%wide.region_11.12_spmd.clone, body=%wide.region_2.11_spmd.clone.sunk | while | flops 140646912 | bytes 5729482 | solution.py:103
  130.6 8.3 %while.64 = (s32[]{:T(128)}, f32[2,512,128]{2,1,0:T(8,128)S(1)}, f32[2,512]{1,0:T(2,128)S(1)}, f32[2,512]{1,0:T(2,128)S(1)}, s32[2,512]{1,0:T(2,128)S(1)}, /*ind...) while((s32[]{:T(128)}, f32[2,512,128]{2,1,0:T(8,128)S(1)}, ...), condition=%wide.region_10.10_spmd.clone.clone.clone, body=%wide.region_3.9_spmd.clone.clone.clone.sunk | while | flops 140643840 | bytes 5200729 | solution.py:82
  139.9 8.3 %while.64 = (s32[]{:T(128)}, f32[2,512,128]{2,1,0:T(8,128)S(1)}, f32[2,512]{1,0:T(2,128)S(1)}, f32[2,512]{1,0:T(2,128)S(1)}, s32[2,512]{1,0:T(2,128)S(1)}, /*ind...) while((s32[]{:T(128)}, f32[2,512,128]{2,1,0:T(8,128)S(1)}, ...), condition=%wide.region_10.10_spmd.clone.clone.clone, body=%wide.region_3.9_spmd.clone.clone.clone.sunk | while | flops 140643840 | bytes 5200729 | solution.py:82
  149.3 8.3 %while.64 = (s32[]{:T(128)}, f32[2,512,128]{2,1,0:T(8,128)S(1)}, f32[2,512]{1,0:T(2,128)S(1)}, f32[2,512]{1,0:T(2,128)S(1)}, s32[2,512]{1,0:T(2,128)S(1)}, /*ind...) while((s32[]{:T(128)}, f32[2,512,128]{2,1,0:T(8,128)S(1)}, ...), condition=%wide.region_10.10_spmd.clone.clone.clone, body=%wide.region_3.9_spmd.clone.clone.clone.sunk | while | flops 140643840 | bytes 5200729 | solution.py:82
  158.6 8.3 %while.64 = (s32[]{:T(128)}, f32[2,512,128]{2,1,0:T(8,128)S(1)}, f32[2,512]{1,0:T(2,128)S(1)}, f32[2,512]{1,0:T(2,128)S(1)}, s32[2,512]{1,0:T(2,128)S(1)}, /*ind...) while((s32[]{:T(128)}, f32[2,512,128]{2,1,0:T(8,128)S(1)}, ...), condition=%wide.region_10.10_spmd.clone.clone.clone, body=%wide.region_3.9_spmd.clone.clone.clone.sunk | while | flops 140643840 | bytes 5200729 | solution.py:82
  167.9 8.3 %while.64 = (s32[]{:T(128)}, f32[2,512,128]{2,1,0:T(8,128)S(1)}, f32[2,512]{1,0:T(2,128)S(1)}, f32[2,512]{1,0:T(2,128)S(1)}, s32[2,512]{1,0:T(2,128)S(1)}, /*ind...) while((s32[]{:T(128)}, f32[2,512,128]{2,1,0:T(8,128)S(1)}, ...), condition=%wide.region_10.10_spmd.clone.clone.clone, body=%wide.region_3.9_spmd.clone.clone.clone.sunk | while | flops 140643840 | bytes 5200729 | solution.py:82
  177.2 8.3 %while.64 = (s32[]{:T(128)}, f32[2,512,128]{2,1,0:T(8,128)S(1)}, f32[2,512]{1,0:T(2,128)S(1)}, f32[2,512]{1,0:T(2,128)S(1)}, s32[2,512]{1,0:T(2,128)S(1)}, /*ind...) while((s32[]{:T(128)}, f32[2,512,128]{2,1,0:T(8,128)S(1)}, ...), condition=%wide.region_10.10_spmd.clone.clone.clone, body=%wide.region_3.9_spmd.clone.clone.clone.sunk | while | flops 140643840 | bytes 5200729 | solution.py:82
  186.6 8.3 %while.64 = (s32[]{:T(128)}, f32[2,512,128]{2,1,0:T(8,128)S(1)}, f32[2,512]{1,0:T(2,128)S(1)}, f32[2,512]{1,0:T(2,128)S(1)}, s32[2,512]{1,0:T(2,128)S(1)}, /*ind...) while((s32[]{:T(128)}, f32[2,512,128]{2,1,0:T(8,128)S(1)}, ...), condition=%wide.region_10.10_spmd.clone.clone.clone, body=%wide.region_3.9_spmd.clone.clone.clone.sunk | while | flops 140643840 | bytes 5200729 | solution.py:82
  195.9 8.3 %while.64 = (s32[]{:T(128)}, f32[2,512,128]{2,1,0:T(8,128)S(1)}, f32[2,512]{1,0:T(2,128)S(1)}, f32[2,512]{1,0:T(2,128)S(1)}, s32[2,512]{1,0:T(2,128)S(1)}, /*ind...) while((s32[]{:T(128)}, f32[2,512,128]{2,1,0:T(8,128)S(1)}, ...), condition=%wide.region_10.10_spmd.clone.clone.clone, body=%wide.region_3.9_spmd.clone.clone.clone.sunk | while | flops 140643840 | bytes 5200729 | solution.py:82
  205.2 8.3 %while.64 = (s32[]{:T(128)}, f32[2,512,128]{2,1,0:T(8,128)S(1)}, f32[2,512]{1,0:T(2,128)S(1)}, f32[2,512]{1,0:T(2,128)S(1)}, s32[2,512]{1,0:T(2,128)S(1)}, /*ind...) while((s32[]{:T(128)}, f32[2,512,128]{2,1,0:T(8,128)S(1)}, ...), condition=%wide.region_10.10_spmd.clone.clone.clone, body=%wide.region_3.9_spmd.clone.clone.clone.sunk | while | flops 140643840 | bytes 5200729 | solution.py:82
  214.5 8.3 %while.64 = (s32[]{:T(128)}, f32[2,512,128]{2,1,0:T(8,128)S(1)}, f32[2,512]{1,0:T(2,128)S(1)}, f32[2,512]{1,0:T(2,128)S(1)}, s32[2,512]{1,0:T(2,128)S(1)}, /*ind...) while((s32[]{:T(128)}, f32[2,512,128]{2,1,0:T(8,128)S(1)}, ...), condition=%wide.region_10.10_spmd.clone.clone.clone, body=%wide.region_3.9_spmd.clone.clone.clone.sunk | while | flops 140643840 | bytes 5200729 | solution.py:82
  223.8 8.3 %while.64 = (s32[]{:T(128)}, f32[2,512,128]{2,1,0:T(8,128)S(1)}, f32[2,512]{1,0:T(2,128)S(1)}, f32[2,512]{1,0:T(2,128)S(1)}, s32[2,512]{1,0:T(2,128)S(1)}, /*ind...) while((s32[]{:T(128)}, f32[2,512,128]{2,1,0:T(8,128)S(1)}, ...), condition=%wide.region_10.10_spmd.clone.clone.clone, body=%wide.region_3.9_spmd.clone.clone.clone.sunk | while | flops 140643840 | bytes 5200729 | solution.py:82
  233.2 8.3 %while.64 = (s32[]{:T(128)}, f32[2,512,128]{2,1,0:T(8,128)S(1)}, f32[2,512]{1,0:T(2,128)S(1)}, f32[2,512]{1,0:T(2,128)S(1)}, s32[2,512]{1,0:T(2,128)S(1)}, /*ind...) while((s32[]{:T(128)}, f32[2,512,128]{2,1,0:T(8,128)S(1)}, ...), condition=%wide.region_10.10_spmd.clone.clone.clone, body=%wide.region_3.9_spmd.clone.clone.clone.sunk | while | flops 140643840 | bytes 5200729 | solution.py:82
  242.5 8.3 %while.64 = (s32[]{:T(128)}, f32[2,512,128]{2,1,0:T(8,128)S(1)}, f32[2,512]{1,0:T(2,128)S(1)}, f32[2,512]{1,0:T(2,128)S(1)}, s32[2,512]{1,0:T(2,128)S(1)}, /*ind...) while((s32[]{:T(128)}, f32[2,512,128]{2,1,0:T(8,128)S(1)}, ...), condition=%wide.region_10.10_spmd.clone.clone.clone, body=%wide.region_3.9_spmd.clone.clone.clone.sunk | while | flops 140643840 | bytes 5200729 | solution.py:82
  251.8 8.3 %while.64 = (s32[]{:T(128)}, f32[2,512,128]{2,1,0:T(8,128)S(1)}, f32[2,512]{1,0:T(2,128)S(1)}, f32[2,512]{1,0:T(2,128)S(1)}, s32[2,512]{1,0:T(2,128)S(1)}, /*ind...) while((s32[]{:T(128)}, f32[2,512,128]{2,1,0:T(8,128)S(1)}, ...), condition=%wide.region_10.10_spmd.clone.clone.clone, body=%wide.region_3.9_spmd.clone.clone.clone.sunk | while | flops 140643840 | bytes 5200729 | solution.py:82
  261.1 8.3 %while.64 = (s32[]{:T(128)}, f32[2,512,128]{2,1,0:T(8,128)S(1)}, f32[2,512]{1,0:T(2,128)S(1)}, f32[2,512]{1,0:T(2,128)S(1)}, s32[2,512]{1,0:T(2,128)S(1)}, /*ind...) while((s32[]{:T(128)}, f32[2,512,128]{2,1,0:T(8,128)S(1)}, ...), condition=%wide.region_10.10_spmd.clone.clone.clone, body=%wide.region_3.9_spmd.clone.clone.clone.sunk | while | flops 140643840 | bytes 5200729 | solution.py:82
  270.5 19.0 %while.64 = (s32[]{:T(128)}, f32[2,512,128]{2,1,0:T(8,128)S(1)}, f32[2,512]{1,0:T(2,128)S(1)}, f32[2,512]{1,0:T(2,128)S(1)}, s32[2,512]{1,0:T(2,128)S(1)}, /*ind...) while((s32[]{:T(128)}, f32[2,512,128]{2,1,0:T(8,128)S(1)}, ...), condition=%wide.region_10.10_spmd.clone.clone.clone, body=%wide.region_3.9_spmd.clone.clone.clone.sunk | while | flops 140643840 | bytes 5200729 | solution.py:82
  283.3 5.4 conditional.5
  290.5 19.0 %while.64 = (s32[]{:T(128)}, f32[2,512,128]{2,1,0:T(8,128)S(1)}, f32[2,512]{1,0:T(2,128)S(1)}, f32[2,512]{1,0:T(2,128)S(1)}, s32[2,512]{1,0:T(2,128)S(1)}, /*ind...) while((s32[]{:T(128)}, f32[2,512,128]{2,1,0:T(8,128)S(1)}, ...), condition=%wide.region_10.10_spmd.clone.clone.clone, body=%wide.region_3.9_spmd.clone.clone.clone.sunk | while | flops 140643840 | bytes 5200729 | solution.py:82
  303.3 5.4 conditional.5
  310.5 19.0 %while.64 = (s32[]{:T(128)}, f32[2,512,128]{2,1,0:T(8,128)S(1)}, f32[2,512]{1,0:T(2,128)S(1)}, f32[2,512]{1,0:T(2,128)S(1)}, s32[2,512]{1,0:T(2,128)S(1)}, /*ind...) while((s32[]{:T(128)}, f32[2,512,128]{2,1,0:T(8,128)S(1)}, ...), condition=%wide.region_10.10_spmd.clone.clone.clone, body=%wide.region_3.9_spmd.clone.clone.clone.sunk | while | flops 140643840 | bytes 5200729 | solution.py:82
  313.8 5.4 conditional.5
  323.3 5.4 conditional.5
  330.5 19.0 %while.64 = (s32[]{:T(128)}, f32[2,512,128]{2,1,0:T(8,128)S(1)}, f32[2,512]{1,0:T(2,128)S(1)}, f32[2,512]{1,0:T(2,128)S(1)}, s32[2,512]{1,0:T(2,128)S(1)}, /*ind...) while((s32[]{:T(128)}, f32[2,512,128]{2,1,0:T(8,128)S(1)}, ...), condition=%wide.region_10.10_spmd.clone.clone.clone, body=%wide.region_3.9_spmd.clone.clone.clone.sunk | while | flops 140643840 | bytes 5200729 | solution.py:82
  333.9 5.4 conditional.5
  343.4 5.4 conditional.5
  350.6 19.0 %while.64 = (s32[]{:T(128)}, f32[2,512,128]{2,1,0:T(8,128)S(1)}, f32[2,512]{1,0:T(2,128)S(1)}, f32[2,512]{1,0:T(2,128)S(1)}, s32[2,512]{1,0:T(2,128)S(1)}, /*ind...) while((s32[]{:T(128)}, f32[2,512,128]{2,1,0:T(8,128)S(1)}, ...), condition=%wide.region_10.10_spmd.clone.clone.clone, body=%wide.region_3.9_spmd.clone.clone.clone.sunk | while | flops 140643840 | bytes 5200729 | solution.py:82
  353.9 5.4 conditional.5
  363.4 5.4 conditional.5
  370.6 19.0 %while.64 = (s32[]{:T(128)}, f32[2,512,128]{2,1,0:T(8,128)S(1)}, f32[2,512]{1,0:T(2,128)S(1)}, f32[2,512]{1,0:T(2,128)S(1)}, s32[2,512]{1,0:T(2,128)S(1)}, /*ind...) while((s32[]{:T(128)}, f32[2,512,128]{2,1,0:T(8,128)S(1)}, ...), condition=%wide.region_10.10_spmd.clone.clone.clone, body=%wide.region_3.9_spmd.clone.clone.clone.sunk | while | flops 140643840 | bytes 5200729 | solution.py:82
  373.9 5.4 conditional.5
  383.4 5.4 conditional.5
  390.6 19.0 %while.64 = (s32[]{:T(128)}, f32[2,512,128]{2,1,0:T(8,128)S(1)}, f32[2,512]{1,0:T(2,128)S(1)}, f32[2,512]{1,0:T(2,128)S(1)}, s32[2,512]{1,0:T(2,128)S(1)}, /*ind...) while((s32[]{:T(128)}, f32[2,512,128]{2,1,0:T(8,128)S(1)}, ...), condition=%wide.region_10.10_spmd.clone.clone.clone, body=%wide.region_3.9_spmd.clone.clone.clone.sunk | while | flops 140643840 | bytes 5200729 | solution.py:82
  393.9 5.4 conditional.5
  403.4 5.4 conditional.5
  410.6 19.0 %while.64 = (s32[]{:T(128)}, f32[2,512,128]{2,1,0:T(8,128)S(1)}, f32[2,512]{1,0:T(2,128)S(1)}, f32[2,512]{1,0:T(2,128)S(1)}, s32[2,512]{1,0:T(2,128)S(1)}, /*ind...) while((s32[]{:T(128)}, f32[2,512,128]{2,1,0:T(8,128)S(1)}, ...), condition=%wide.region_10.10_spmd.clone.clone.clone, body=%wide.region_3.9_spmd.clone.clone.clone.sunk | while | flops 140643840 | bytes 5200729 | solution.py:82
  414.0 5.4 conditional.5
  423.5 5.4 conditional.5
  430.7 19.0 %while.64 = (s32[]{:T(128)}, f32[2,512,128]{2,1,0:T(8,128)S(1)}, f32[2,512]{1,0:T(2,128)S(1)}, f32[2,512]{1,0:T(2,128)S(1)}, s32[2,512]{1,0:T(2,128)S(1)}, /*ind...) while((s32[]{:T(128)}, f32[2,512,128]{2,1,0:T(8,128)S(1)}, ...), condition=%wide.region_10.10_spmd.clone.clone.clone, body=%wide.region_3.9_spmd.clone.clone.clone.sunk | while | flops 140643840 | bytes 5200729 | solution.py:82
  434.0 5.4 conditional.5
  443.5 5.4 conditional.5
  450.7 19.0 %while.64 = (s32[]{:T(128)}, f32[2,512,128]{2,1,0:T(8,128)S(1)}, f32[2,512]{1,0:T(2,128)S(1)}, f32[2,512]{1,0:T(2,128)S(1)}, s32[2,512]{1,0:T(2,128)S(1)}, /*ind...) while((s32[]{:T(128)}, f32[2,512,128]{2,1,0:T(8,128)S(1)}, ...), condition=%wide.region_10.10_spmd.clone.clone.clone, body=%wide.region_3.9_spmd.clone.clone.clone.sunk | while | flops 140643840 | bytes 5200729 | solution.py:82
  454.0 5.4 conditional.5
  463.5 5.4 conditional.5
  470.7 19.0 %while.64 = (s32[]{:T(128)}, f32[2,512,128]{2,1,0:T(8,128)S(1)}, f32[2,512]{1,0:T(2,128)S(1)}, f32[2,512]{1,0:T(2,128)S(1)}, s32[2,512]{1,0:T(2,128)S(1)}, /*ind...) while((s32[]{:T(128)}, f32[2,512,128]{2,1,0:T(8,128)S(1)}, ...), condition=%wide.region_10.10_spmd.clone.clone.clone, body=%wide.region_3.9_spmd.clone.clone.clone.sunk | while | flops 140643840 | bytes 5200729 | solution.py:82
  474.0 5.4 conditional.5
  483.5 5.4 conditional.5
  490.7 19.0 %while.64 = (s32[]{:T(128)}, f32[2,512,128]{2,1,0:T(8,128)S(1)}, f32[2,512]{1,0:T(2,128)S(1)}, f32[2,512]{1,0:T(2,128)S(1)}, s32[2,512]{1,0:T(2,128)S(1)}, /*ind...) while((s32[]{:T(128)}, f32[2,512,128]{2,1,0:T(8,128)S(1)}, ...), condition=%wide.region_10.10_spmd.clone.clone.clone, body=%wide.region_3.9_spmd.clone.clone.clone.sunk | while | flops 140643840 | bytes 5200729 | solution.py:82
  494.1 5.4 conditional.5
  503.6 5.4 conditional.5
  510.8 19.0 %while.64 = (s32[]{:T(128)}, f32[2,512,128]{2,1,0:T(8,128)S(1)}, f32[2,512]{1,0:T(2,128)S(1)}, f32[2,512]{1,0:T(2,128)S(1)}, s32[2,512]{1,0:T(2,128)S(1)}, /*ind...) while((s32[]{:T(128)}, f32[2,512,128]{2,1,0:T(8,128)S(1)}, ...), condition=%wide.region_10.10_spmd.clone.clone.clone, body=%wide.region_3.9_spmd.clone.clone.clone.sunk | while | flops 140643840 | bytes 5200729 | solution.py:82
  514.1 5.4 conditional.5
  523.6 5.4 conditional.5
  530.8 19.0 %while.64 = (s32[]{:T(128)}, f32[2,512,128]{2,1,0:T(8,128)S(1)}, f32[2,512]{1,0:T(2,128)S(1)}, f32[2,512]{1,0:T(2,128)S(1)}, s32[2,512]{1,0:T(2,128)S(1)}, /*ind...) while((s32[]{:T(128)}, f32[2,512,128]{2,1,0:T(8,128)S(1)}, ...), condition=%wide.region_10.10_spmd.clone.clone.clone, body=%wide.region_3.9_spmd.clone.clone.clone.sunk | while | flops 140643840 | bytes 5200729 | solution.py:82
  534.1 5.4 conditional.5
  550.8 19.0 %while.64 = (s32[]{:T(128)}, f32[2,512,128]{2,1,0:T(8,128)S(1)}, f32[2,512]{1,0:T(2,128)S(1)}, f32[2,512]{1,0:T(2,128)S(1)}, s32[2,512]{1,0:T(2,128)S(1)}, /*ind...) while((s32[]{:T(128)}, f32[2,512,128]{2,1,0:T(8,128)S(1)}, ...), condition=%wide.region_10.10_spmd.clone.clone.clone, body=%wide.region_3.9_spmd.clone.clone.clone.sunk | while | flops 140643840 | bytes 5200729 | solution.py:82
  554.1 5.4 conditional.5
  570.8 19.0 %while.64 = (s32[]{:T(128)}, f32[2,512,128]{2,1,0:T(8,128)S(1)}, f32[2,512]{1,0:T(2,128)S(1)}, f32[2,512]{1,0:T(2,128)S(1)}, s32[2,512]{1,0:T(2,128)S(1)}, /*ind...) while((s32[]{:T(128)}, f32[2,512,128]{2,1,0:T(8,128)S(1)}, ...), condition=%wide.region_10.10_spmd.clone.clone.clone, body=%wide.region_3.9_spmd.clone.clone.clone.sunk | while | flops 140643840 | bytes 5200729 | solution.py:82
  574.2 5.4 conditional.5
  590.9 13.6 %while.64 = (s32[]{:T(128)}, f32[2,512,128]{2,1,0:T(8,128)S(1)}, f32[2,512]{1,0:T(2,128)S(1)}, f32[2,512]{1,0:T(2,128)S(1)}, s32[2,512]{1,0:T(2,128)S(1)}, /*ind...) while((s32[]{:T(128)}, f32[2,512,128]{2,1,0:T(8,128)S(1)}, ...), condition=%wide.region_10.10_spmd.clone.clone.clone, body=%wide.region_3.9_spmd.clone.clone.clone.sunk | while | flops 140643840 | bytes 5200729 | solution.py:82
  (861 shorter events, 422.0 us)
Async XLA Ops:
  6.5 81.9 %all-gather.7.cloned.1.call-start = ((), (), s32[]{:S(2)}) async-start(), calls=%async_computation.1 | async-start | bytes 4456448 | tf_op jit(solution)/shard_map/all_gather | solution.py:153
  46.3 83.3 %all-gather.5.cloned.1.call-start = ((), (), s32[]{:S(2)}) async-start(), calls=%async_computation | async-start | bytes 4456448 | tf_op jit(solution)/shard_map/all_gather | solution.py:152
Sparse Core Ops, SparseCore 0:
  46.4 42.0 all-gather.6
  90.3 39.1 all-gather.4
where the time goes:
time: 620 us; the launch traced here: 612 us
  local copies, waits for them, and re-layouts  166 us (27%)
  other arithmetic  128 us (21%)
  matrix products  95.1 us (15%)
  loops' own time  89.4 us (14%)
  blocking collectives  71.4 us (12%)
  waiting for transfers between devices  48.4 us (8%)
  between operations  13.4 us (2%)
    another operation x32, loops' own time, update_state(): lax.map(per_block, (query_blocks, pos_blocks, first_blocks) + tuple(one_s...  86.6 us
    dynamic_update_slice x192, local copies, waits for them, and re-layouts, update_state(): lax.map(per_block, (query_blocks, pos_blocks, first_blocks) + tuple(one_s...  50.2 us
    dot_general x33, matrix products, attend(): jnp.dot(weights.astype(jnp.bfloat16), value_rows, preferred_element_type=...  49.4 us
    dot_general x33, matrix products, attend(): jnp.einsum('rd,kd->rk', query_rows, key_rows, preferred_element_type=jnp....  45.7 us
    reduce_min x64, other arithmetic, per_block(): jnp.min(query_first)  45.3 us
    while x64, local copies, waits for them, and re-layouts  43.7 us
    all_gather x1, waiting for transfers between devices, local(): lax.all_gather(group_keys, 'seq', axis=0, tiled=True)  41.1 us
    all_gather x1, blocking collectives, local(): lax.all_gather(value_heads, 'head', axis=1, tiled=True)  39 us
  transfers between devices with their start and end apart: 2, of which 2 were waited for; matrix products, arithmetic and copies ran while one was open for 0% of the time, Pallas kernels for 0%

commit v1 on v0

v1 whole, which is shorter than its diff:
```python
import functools
import math

import jax
import jax.numpy as jnp
from jax import lax
from jax.experimental import pallas as pl
from jax.experimental.pallas import tpu as pltpu
from jax.sharding import PartitionSpec as P

QH = 16
KVH = 2
HIDDEN = -1e30
LOG_SCALE = math.log2(math.e) / math.sqrt(128)
NT = (((1,), (1,)), ((), ()))
NN = (((1,), (0,)), ((), ()))


def attention_kernel(block, chunk, doc_ref, q_ref, kv_ref, o_ref, acc, peak, total, first):
    rows = q_ref.shape[0]
    start = lax.axis_index("seq") * rows
    peak[...] = jnp.full_like(peak, HIDDEN)
    total[...] = jnp.zeros_like(total)
    acc[...] = jnp.zeros_like(acc)
    pos = start + lax.broadcasted_iota(jnp.int32, (rows, 128), 0)
    doc_first = jnp.zeros((rows, 128), jnp.int32)
    low = jnp.int32(0)
    begin = jnp.int32(0)
    for d in range(doc_ref.shape[0]):
        doc_first = jnp.where(pos >= begin, begin, doc_first)
        low = jnp.where(start >= begin, begin, low)
        begin = begin + doc_ref[d]
    first[...] = doc_first

    def step(j, carry):
        base = pl.multiple_of(j * chunk, chunk)
        keys = kv_ref[0, pl.ds(base, chunk), :]
        values = kv_ref[1, pl.ds(base, chunk), :]
        lane = base + lax.broadcasted_iota(jnp.int32, (block, 128), 1)

        def score(i):
            return lax.dot_general(q_ref[pl.ds(i * block, block), :], keys, NT, preferred_element_type=jnp.float32)

        count = rows // block
        ahead = score(0)
        for i in range(count):
            s = ahead
            ahead = score(i + 1) if i + 1 < count else None
            r = pl.ds(i * block, block)
            f = first[r, :]
            line = start + i * block + lax.broadcasted_iota(jnp.int32, (block, 128), 0)
            cols = []
            for g in range(chunk // 128):
                key_pos = lane + g * 128
                cols.append(jnp.where((key_pos >= f) & (key_pos <= line), s[:, g * 128:(g + 1) * 128], HIDDEN))
            top = cols
            while len(top) > 1:
                top = [jnp.maximum(a, b) for a, b in zip(top[::2], top[1::2])]
            old = peak[r, :]
            new = jnp.maximum(old, jnp.max(top[0], axis=1, keepdims=True))
            shift = new * LOG_SCALE
            factor = jnp.exp2(old * LOG_SCALE - shift)
            peak[r, :] = new
            weights = [jnp.exp2(c * LOG_SCALE - shift) for c in cols]
            summed = weights
            while len(summed) > 1:
                summed = [a + b for a, b in zip(summed[::2], summed[1::2])]
            total[r, :] = total[r, :] * factor + summed[0]
            p = jnp.concatenate([w.astype(jnp.bfloat16) for w in weights], axis=1)
            acc[r, :] = acc[r, :] * factor + lax.dot_general(p, values, NN, preferred_element_type=jnp.float32)
        return carry

    lax.fori_loop(low // chunk, (start + rows) // chunk, step, 0)
    o_ref[...] = (acc[...] / jnp.sum(total[...], axis=1, keepdims=True)).astype(o_ref.dtype)


def local(query_heads, key_heads, value_heads, doc_lengths):
    heads_here, rows, width = query_heads.shape
    head_group = lax.axis_index("head") * heads_here // (QH // KVH)
    both = jnp.stack([key_heads, value_heads], axis=1)
    both = lax.all_gather(both, "head", axis=2, tiled=True)
    both = lax.dynamic_index_in_dim(both, head_group, 0, keepdims=False)
    both = lax.all_gather(both, "seq", axis=1, tiled=True)
    vmem = pl.BlockSpec(memory_space=pltpu.VMEM)
    out = pl.pallas_call(
        functools.partial(attention_kernel, 256, 1024),
        out_shape=jax.ShapeDtypeStruct((rows, width), jnp.bfloat16),
        in_specs=[pl.BlockSpec(memory_space=pltpu.SMEM), vmem, vmem],
        out_specs=vmem,
        scratch_shapes=[
            pltpu.VMEM((rows, width), jnp.float32),
            pltpu.VMEM((rows, 128), jnp.float32),
            pltpu.VMEM((rows, 128), jnp.float32),
            pltpu.VMEM((rows, 128), jnp.int32),
        ],
        compiler_params=pltpu.CompilerParams(vmem_limit_bytes=48 * 2**20),
        name="attention",
    )(doc_lengths, query_heads[0], both)
    return out[None]


def solution(mesh):
    placed = (
        P("head", "seq", None),
        P(None, ("seq", "head"), None),
        P(None, ("seq", "head"), None),
        P(),
    )
    return jax.shard_map(
        local, mesh=mesh, in_specs=placed, out_specs=P("head", "seq", None), check_vma=False
    )
```

time: 620 us -> 180 us (0.29)
  the two profiles are of different devices: /device:TPU:27 before, /device:TPU:10 now
where the time goes in v1:
time: 180 us
  waiting for transfers between devices  135 us (75%)
  Pallas kernels  26.8 us (15%)
  between operations  13.4 us (7%)
  local copies, waits for them, and re-layouts  3.51 us (2%)
    all_gather x1, waiting for transfers between devices, local(): both = lax.all_gather(both, 'head', axis=2, tiled=True)  82.8 us
    all_gather x1, waiting for transfers between devices, local(): both = lax.all_gather(both, 'seq', axis=1, tiled=True)  52.2 us
    pallas_call x1, Pallas kernels, local(): pl.pallas_call(functools.partial(attention_kernel, 256, 1024), out_shape=...  26.8 us
  transfers between devices with their start and end apart: 2, of which 2 were waited for; matrix products, arithmetic and copies ran while one was open for 0% of the time, Pallas kernels for 0%

profile of v1, /device:TPU:10, one launch (start us, length us, event | category | flops | bytes accessed | tf_op | source)
XLA Modules:
  0.0 180.2 jit_solution(3203164865349117470)
XLA Ops:
  6.5 0.0 all-gather.4.cloned.1.call-start
  6.5 1.4 pad_maximum_fusion
  7.9 0.0 all-gather.4.cloned.1.call-update
  8.0 0.0 all-gather.6.cloned.1.call-start
  8.0 82.8 %all-gather.4.cloned.1.call-done = bf16[2,2,1024,128]{3,2,1,0:T(8,128)(2,1)} async-done(((bf16[2,2,64,128]{3,2,1,0:T(8,128)(2,1)}), bf16[2,2,1024,128]{3,2,1,0:T(8,128)(2,1)}) %all-gather.4.cloned.1.call-update) | async-done | bytes 1048592 | tf_op jit(solution)/shard_map/all_gather | solution.py:81
  90.8 1.9 %constant_dynamic-slice_fusion = bf16[1,2,1024,128]{3,2,1,0:T(8,128)(2,1)} fusion(bf16[2,2,1024,128]{3,2,1,0:T(8,128)(2,1)} %all-gather.4.cloned.1.call-done, s32[]{:T(128)S(6)} %select_n.10), kind=kLoop, calls=%fused_computation.1 | loop fusion | bytes 1048580 | tf_op jit(solution)/shard_map/jit(dynamic_index_in_dim)/dynamic_slice | solution.py:82
  92.7 0.0 all-gather.6.cloned.1.call-update
  92.8 52.2 %all-gather.6.cloned.1.call-done = bf16[1,2,16384,128]{3,2,1,0:T(8,128)(2,1)} async-done(((bf16[1,2,1024,128]{3,2,1,0:T(8,128)(2,1)}), bf16[1,2,16384,128]{3,2,1,0:T(8,128)(2,1)}) %all-gather.6.cloned.1.call-update) | async-done | bytes 8388624 | tf_op jit(solution)/shard_map/all_gather | solution.py:83
  145.0 0.0 copy-start
  145.0 0.9 copy-done
  145.9 0.0 copy-start.1
  145.9 0.7 copy-done.1
  146.6 26.8 %attention.1 = bf16[1024,128]{1,0:T(8,128)(2,1)} custom-call(s32[16]{0:T(128)S(1)} %copy-done.1, bf16[1024,128]{1,0:T(8,128)(2,1)S(1)} %bitcast.5, bf16[2,16384,128]{2,1,0:T(8,128)(2,1)} %bitcast.6), custom_call_target="tpu_custom_call" | custom-call | tf_op jit(solution)/shard_map/attention/pallas_call | solution.py:85
Async XLA Ops:
  6.5 84.3 %all-gather.4.cloned.1.call-start = ((), (), s32[]{:S(2)}) async-start(), calls=%async_computation | async-start | bytes 1114112 | tf_op jit(solution)/shard_map/all_gather | solution.py:81
  8.0 137.0 %all-gather.6.cloned.1.call-start = ((), (), s32[]{:S(2)}) async-start(), calls=%async_computation.1 | async-start | bytes 8912896 | tf_op jit(solution)/shard_map/all_gather | solution.py:83
  145.0 0.9 copy-start
  145.9 0.7 copy-start.1
Sparse Core Ops, SparseCore 0:
  10.0 80.8 all-gather.3
  92.9 52.0 all-gather.5

commit v2 on v1

v2 whole, which is shorter than its diff:
```python
import math

import jax
import jax.numpy as jnp
from jax import lax
from jax.experimental import pallas as pl
from jax.experimental.pallas import tpu as pltpu
from jax.sharding import PartitionSpec as P

HIDDEN = -1e30
FAR = -(1 << 20)
LOG_SCALE = math.log2(math.e) / math.sqrt(128)
NT = (((1,), (1,)), ((), ()))
NN = (((1,), (0,)), ((), ()))
MESH = pl.DeviceIdType.MESH

SHARD = 1024
PIECE = 64
UNIT = 2 * PIECE
BLOCK = 256
OWN, OPPOSITE, BEHIND, AHEAD, ACROSS = range(5)
BACK = (0, 2, 1, 3, 4)
OFFSETS = (0, -1, 1, -2, 2, -3, 3, -4)
ROUNDS = ((0,), (1, 2), (3, 4), (5, 6), (7,))


def attention_kernel(
    doc_ref, q_ref, k_ref, v_ref, o_ref,
    even, odd, parcel, acc, peak, total, first,
    swap_sem, own_sem, opposite_sem, across_sem, behind_sem, ahead_sem, turn_sem, core_sem,
):
    seq, head = lax.axis_index("seq"), lax.axis_index("head")
    core, y, x = lax.rem(seq, 2), lax.rem(seq // 2, 4), seq // 8
    z, half = lax.rem(head, 8), head // 8

    def at(x_to, y_to, core_to=core):
        return ((x_to * 4 + y_to) * 2 + core_to, head)

    y_up, y_down = lax.rem(y + 1, 4), lax.rem(y + 3, 4)
    swap_to = (seq, (1 - half) * 8 + z)
    z_up_to = (seq, half * 8 + lax.rem(z + 1, 8))
    z_down_to = (seq, half * 8 + lax.rem(z + 7, 8))
    across_to = at(1 - x, y)
    up_to, down_to, turn_to = at(x, y_up), at(x, y_down), at(x, lax.rem(y + 2, 4))
    core_to = at(x, y, 1 - core)

    barrier = pltpu.get_barrier_semaphore()
    partners = (swap_to, z_up_to, z_down_to, across_to, up_to, down_to, turn_to, core_to)
    for partner in partners:
        pl.semaphore_signal(barrier, inc=1, device_id=partner, device_id_type=MESH)

    parcel[0] = k_ref[1 - half]
    parcel[1] = v_ref[1 - half]
    mine = pl.ds(pl.multiple_of(half * PIECE, PIECE), PIECE)
    even[z, OWN, 0, mine, :] = k_ref[half]
    even[z, OWN, 1, mine, :] = v_ref[half]
    pl.semaphore_wait(barrier, len(partners))

    slice_of = [lax.rem(z + off + 8, 8) for off in OFFSETS]

    def copy(src, dst, sems, index, to):
        return pltpu.make_async_remote_copy(
            src_ref=src, dst_ref=dst, send_sem=sems.at[0, index], recv_sem=sems.at[1, index],
            device_id=to, device_id_type=MESH,
        )

    swap_out = copy(parcel, even.at[z, OWN, :, mine, :], swap_sem, 0, swap_to)
    theirs = pl.ds(pl.multiple_of((1 - half) * PIECE, PIECE), PIECE)
    swap_in = copy(parcel, even.at[z, OWN, :, theirs, :], swap_sem, 0, swap_to)
    swap_out.start()

    def ring(slot, sems, u, unit, to):
        ref = even.at[slice_of[unit], slot]
        return copy(ref, ref, sems, u - 1, to)

    def ring_in(slot, sems, u):
        return ring(slot, sems, u, u, z_up_to)

    def ring_out(slot, sems, unit):
        out = []
        if OFFSETS[unit] <= 0 and OFFSETS[unit] > -4:
            u = OFFSETS.index(OFFSETS[unit] - 1)
            out.append(ring(slot, sems, u, unit, z_up_to))
        if OFFSETS[unit] >= 0 and OFFSETS[unit] < 3:
            u = OFFSETS.index(OFFSETS[unit] + 1)
            out.append(ring(slot, sems, u, unit, z_down_to))
        return out

    def across(u):
        return copy(even.at[slice_of[u], OWN], even.at[slice_of[u], ACROSS], across_sem, u, across_to)

    up_slot = jnp.where(y == 3, ACROSS, OWN)
    down_slot = jnp.where(y == 0, OWN, ACROSS)
    turn_slot = jnp.where(y < 2, OWN, ACROSS)

    def up(u):
        return copy(even.at[slice_of[u], up_slot], even.at[slice_of[u], BEHIND], behind_sem, u, up_to)

    def down(u):
        return copy(even.at[slice_of[u], down_slot], even.at[slice_of[u], AHEAD], ahead_sem, u, down_to)

    turn = copy(even.at[z, turn_slot], even.at[z, OPPOSITE], turn_sem, 0, turn_to)

    def to_core(u):
        return copy(even.at[slice_of[u], pl.ds(core, 4)], odd.at[slice_of[u]], core_sem, u, core_to)

    started = [swap_out]

    def send(copies):
        for one in copies:
            one.start()
            started.append(one)

    def own_arrives(step):
        for u in ROUNDS[step]:
            if u == 0:
                swap_in.wait_recv()
            else:
                ring_in(OWN, own_sem, u).wait_recv()
            send(ring_out(OWN, own_sem, u))
            send([across(u)])

    def across_arrives(step):
        for u in ROUNDS[step]:
            across(u).wait_recv()
            send([up(u), down(u)])
            if u == 0:
                send([turn])

    def opposite_arrives(step):
        for u in ROUNDS[step]:
            if u == 0:
                turn.wait_recv()
            else:
                ring_in(OPPOSITE, opposite_sem, u).wait_recv()
            send(ring_out(OPPOSITE, opposite_sem, u))

    def sides_arrive(step):
        for u in ROUNDS[step]:
            up(u).wait_recv()
            down(u).wait_recv()
            send([to_core(u)])

    def core_arrives(step):
        for u in ROUNDS[step]:
            to_core(u).wait_recv()

    chip = x * 4 + y
    start = seq * SHARD
    lane = lax.broadcasted_iota(jnp.int32, (1, 128), 1)
    place = jnp.where(lane < PIECE, lane, lane + (SHARD // 2 - PIECE))

    def base(slot, u, from_sibling):
        if from_sibling:
            back = jnp.where(core == 1, BACK[slot], BACK[slot + 1])
            owner = chip - back
            shard = owner * 2 + (1 - core)
        else:
            owner = chip - BACK[slot]
            shard = owner * 2 + core
        return jnp.where(owner >= 0, shard * SHARD + slice_of[u] * PIECE, FAR)

    def attend(keys, values, bases, causal, blocks):
        groups = len(bases)

        def score(i):
            return lax.dot_general(q_ref[0, pl.ds(i * BLOCK, BLOCK), :], keys, NT, preferred_element_type=jnp.float32)

        ahead = score(blocks[0])
        for n, i in enumerate(blocks):
            s = ahead
            ahead = score(blocks[n + 1]) if n + 1 < len(blocks) else None
            r = pl.ds(i * BLOCK, BLOCK)
            f = first[r, :]
            if causal:
                line = start + i * BLOCK + lax.broadcasted_iota(jnp.int32, (BLOCK, 128), 0) - place
            cols = []
            for g in range(groups):
                seen = f <= bases[g]
                if causal:
                    seen = seen & (line >= bases[g])
                cols.append(jnp.where(seen, s[:, g * UNIT:(g + 1) * UNIT], HIDDEN))
            top = tree(jnp.maximum, cols)
            old = peak[r, :]
            new = jnp.maximum(old, jnp.max(top, axis=1, keepdims=True))
            shift = new * LOG_SCALE
            factor = jnp.exp2(old * LOG_SCALE - shift)
            peak[r, :] = new
            weights = [jnp.exp2(c * LOG_SCALE - shift) for c in cols]
            total[r, :] = total[r, :] * factor + tree(jnp.add, weights)
            p = jnp.concatenate([w.astype(jnp.bfloat16) for w in weights], axis=1)
            acc[r, :] = acc[r, :] * factor + lax.dot_general(p, values, NN, preferred_element_type=jnp.float32)

    def attend_own(units):
        keys = jnp.concatenate([even[slice_of[u], OWN, 0] for u in units], axis=0)
        values = jnp.concatenate([even[slice_of[u], OWN, 1] for u in units], axis=0)
        attend(keys, values, [base(OWN, u, False) for u in units], True, (0, 1, 2, 3))

    def attend_others(step, blocks=(0, 1, 2, 3)):
        keys, values, bases = [], [], []
        for u in ROUNDS[step]:
            for ref, slots, sibling in ((even, range(1, 5), False), (odd, range(4), True)):
                for slot in slots:
                    keys.append(ref[slice_of[u], slot, 0])
                    values.append(ref[slice_of[u], slot, 1])
                    bases.append(base(slot, u, sibling))
        attend(jnp.concatenate(keys, axis=0), jnp.concatenate(values, axis=0), bases, False, blocks)

    peak[...] = jnp.full_like(peak, HIDDEN)
    total[...] = jnp.zeros_like(total)
    acc[...] = jnp.zeros_like(acc)
    pos = start + lax.broadcasted_iota(jnp.int32, (SHARD, 128), 0)
    doc_first = jnp.zeros((SHARD, 128), jnp.int32)
    begin = jnp.int32(0)
    for d in range(doc_ref.shape[0]):
        doc_first = jnp.where(pos >= begin, begin, doc_first)
        begin = begin + doc_ref[d]
    first[...] = doc_first - place

    own_arrives(0)
    across_arrives(0)
    own_arrives(1)
    attend_own((0, 1, 2))
    opposite_arrives(0)
    across_arrives(1)
    own_arrives(2)
    sides_arrive(0)
    opposite_arrives(1)
    across_arrives(2)
    own_arrives(3)
    core_arrives(0)
    attend_others(0)
    sides_arrive(1)
    opposite_arrives(2)
    across_arrives(3)
    own_arrives(4)
    attend_own((3, 4, 5, 6, 7))
    core_arrives(1)
    attend_others(1, (0, 1))
    sides_arrive(2)
    opposite_arrives(3)
    across_arrives(4)
    attend_others(1, (2, 3))
    sides_arrive(3)
    opposite_arrives(4)
    core_arrives(2)
    attend_others(2)
    sides_arrive(4)
    core_arrives(3)
    attend_others(3)
    core_arrives(4)
    attend_others(4)
    o_ref[0] = (acc[...] / jnp.sum(total[...], axis=1, keepdims=True)).astype(o_ref.dtype)
    for one in started:
        one.wait_send()


def tree(join, parts):
    while len(parts) > 1:
        rest = [parts[-1]] if len(parts) % 2 else []
        parts = [join(a, b) for a, b in zip(parts[::2], parts[1::2])] + rest
    return parts[0]


def local(query_heads, key_heads, value_heads, doc_lengths):
    _, rows, width = query_heads.shape
    vmem = pl.BlockSpec(memory_space=pltpu.VMEM)

    def sems(n):
        return pltpu.SemaphoreType.DMA((2, n))

    return pl.pallas_call(
        attention_kernel,
        out_shape=jax.ShapeDtypeStruct(query_heads.shape, jnp.bfloat16),
        in_specs=[pl.BlockSpec(memory_space=pltpu.SMEM), vmem, vmem, vmem],
        out_specs=vmem,
        scratch_shapes=[
            pltpu.VMEM((8, 5, 2, UNIT, width), jnp.bfloat16),
            pltpu.VMEM((8, 4, 2, UNIT, width), jnp.bfloat16),
            pltpu.VMEM((2, PIECE, width), jnp.bfloat16),
            pltpu.VMEM((rows, width), jnp.float32),
            pltpu.VMEM((rows, 128), jnp.float32),
            pltpu.VMEM((rows, 128), jnp.float32),
            pltpu.VMEM((rows, 128), jnp.int32),
            sems(1), sems(7), sems(7), sems(8), sems(8), sems(8), sems(1), sems(8),
        ],
        compiler_params=pltpu.CompilerParams(
            collective_id=0, has_side_effects=True, vmem_limit_bytes=48 * 2**20
        ),
        name="attention",
    )(doc_lengths, query_heads, key_heads, value_heads)


def solution(mesh):
    placed = (
        P("head", "seq", None),
        P(None, ("seq", "head"), None),
        P(None, ("seq", "head"), None),
        P(),
    )
    return jax.shard_map(
        local, mesh=mesh, in_specs=placed, out_specs=P("head", "seq", None), check_vma=False
    )
```

time: 180 us -> 51.1 us (0.28)
  the two profiles are of different devices: /device:TPU:10 before, /device:TPU:8 now
where the time goes in v2:
time: 51.1 us; the launch traced here: 50.4 us
  Pallas kernels  46.6 us (91%)
  local copies, waits for them, and re-layouts  3.82 us (7%)
    pallas_call x1, Pallas kernels, local(): pl.pallas_call(attention_kernel, out_shape=jax.ShapeDtypeStruct(query_hea...  46.6 us
    unnamed x9, local copies, waits for them, and re-layouts  3.82 us

profile of v2, /device:TPU:8, one launch (start us, length us, event | category | flops | bytes accessed | tf_op | source)
XLA Modules:
  0.0 50.4 jit_solution(3488131236810270759)
XLA Ops:
  0.0 0.0 copy-start
  0.0 0.9 %copy-done = bf16[1,1024,128]{2,1,0:T(8,128)(2,1)S(1)} copy-done((bf16[1,1024,128]{2,1,0:T(8,128)(2,1)S(1)}, bf16[1,1024,128]{2,1,0:T(8,128)(2,1)}, u32[]{:S(2)}) %copy-start) | copy-done | bytes 262168
  1.0 0.0 copy-start.1
  1.0 0.8 %copy-done.1 = bf16[2,64,128]{2,1,0:T(8,128)(2,1)S(1)} copy-done((bf16[2,64,128]{2,1,0:T(8,128)(2,1)S(1)}, bf16[2,64,128]{2,1,0:T(8,128)(2,1)}, u32[]{:S(2)}) %copy-start.1) | copy-done | bytes 32792
  1.7 0.0 copy-start.2
  1.7 0.8 %copy-done.2 = bf16[2,64,128]{2,1,0:T(8,128)(2,1)S(1)} copy-done((bf16[2,64,128]{2,1,0:T(8,128)(2,1)S(1)}, bf16[2,64,128]{2,1,0:T(8,128)(2,1)}, u32[]{:S(2)}) %copy-start.2) | copy-done | bytes 32792
  2.5 0.0 copy-start.3
  2.5 0.7 %copy-done.3 = s32[16]{0:T(128)S(1)} copy-done((s32[16]{0:T(128)S(1)}, s32[16]{0:T(128)}, u32[]{:S(2)}) %copy-start.3) | copy-done | bytes 88
  3.1 46.6 %attention.1 = bf16[1,1024,128]{2,1,0:T(8,128)(2,1)S(1)} custom-call(s32[16]{0:T(128)S(1)} %copy-done.3, bf16[1,1024,128]{2,1,0:T(8,128)(2,1)S(1)} %copy-done, bf16[2,64,128]{2,1,0:T(8,128)(2,1)S(1)} %copy-done.1, bf16[2,64,128]{2,1,0:T(8,128)(2,1)S(1)} %copy-done.2), custom_call_target="tpu_custom_call" | custom-call | tf_op jit(solution)/shard_map/attention/pallas_call | solution.py:272
  49.7 0.7 %copy.6 = bf16[1,1024,128]{2,1,0:T(8,128)(2,1)} copy(bf16[1,1024,128]{2,1,0:T(8,128)(2,1)S(1)} %attention.1) | data formatting | bytes 524288
Async XLA Ops:
  0.0 0.9 %copy-start = (bf16[1,1024,128]{2,1,0:T(8,128)(2,1)S(1)}, bf16[1,1024,128]{2,1,0:T(8,128)(2,1)}, u32[]{:S(2)}) copy-start(bf16[1,1024,128]{2,1,0:T(8,128)(2,1)} %q_ref.1) | copy-start | bytes 786436
  1.0 0.8 %copy-start.1 = (bf16[2,64,128]{2,1,0:T(8,128)(2,1)S(1)}, bf16[2,64,128]{2,1,0:T(8,128)(2,1)}, u32[]{:S(2)}) copy-start(bf16[2,64,128]{2,1,0:T(8,128)(2,1)} %k_ref.1) | copy-start | bytes 98308
  1.7 0.8 %copy-start.2 = (bf16[2,64,128]{2,1,0:T(8,128)(2,1)S(1)}, bf16[2,64,128]{2,1,0:T(8,128)(2,1)}, u32[]{:S(2)}) copy-start(bf16[2,64,128]{2,1,0:T(8,128)(2,1)} %v_ref.1) | copy-start | bytes 98308
  2.5 0.7 %copy-start.3 = (s32[16]{0:T(128)S(1)}, s32[16]{0:T(128)}, u32[]{:S(2)}) copy-start(s32[16]{0:T(128)} %doc_ref.1) | copy-start | bytes 196

commit v3 on v2

v3 whole, which is shorter than its diff:
```python
import math

import jax
import jax.numpy as jnp
from jax import lax
from jax.experimental import pallas as pl
from jax.experimental.pallas import tpu as pltpu
from jax.sharding import PartitionSpec as P

HIDDEN = -1e30
FAR = -(1 << 20)
LOG_SCALE = math.log2(math.e) / math.sqrt(128)
NT = (((1,), (1,)), ((), ()))
NN = (((1,), (0,)), ((), ()))
MESH = pl.DeviceIdType.MESH

SHARD = 1024
PIECE = 64
UNIT = 2 * PIECE
BLOCK = 256
OWN, OPPOSITE, BEHIND, AHEAD, ACROSS = range(5)
BACK = (0, 2, 1, 3, 4)
OFFSETS = (0, -1, 1, -2, 2, -3, 3, -4)
ROUNDS = ((0,), (1, 2), (3, 4), (5, 6), (7,))


def attention_kernel(
    doc_ref, q_hbm, k_hbm, v_hbm, o_ref,
    even, odd, parcel, q_ref, acc, peak, total, first,
    load_sem, piece_sem, opposite_sem, relay_sem, start_sem, across_sem, behind_sem, ahead_sem, core_sem,
):
    seq, head = lax.axis_index("seq"), lax.axis_index("head")
    core, y, x = lax.rem(seq, 2), lax.rem(seq // 2, 4), seq // 8
    z, half = lax.rem(head, 8), head // 8
    chip = x * 4 + y
    halves = (half, 1 - half)

    def at(chip_to, core_to, half_to, z_to):
        return (lax.rem(chip_to, 8) * 2 + core_to, half_to * 8 + lax.rem(z_to, 8))

    def along(off):
        return at(chip, core, half, z + (off + 8))

    swap_to = at(chip, core, 1 - half, z)
    across_to = at(chip + 4, core, half, z)
    opposite_to = at(chip + 2, core, half, z)
    opposite_from = at(chip + 6, core, half, z)
    up_to = at(x * 4 + lax.rem(y + 1, 4), core, half, z)
    down_to = at(x * 4 + lax.rem(y + 3, 4), core, half, z)
    core_to = at(chip, 1 - core, half, z)

    mine = pl.ds(pl.multiple_of(half * PIECE, PIECE), PIECE)
    theirs = pl.ds(pl.multiple_of((1 - half) * PIECE, PIECE), PIECE)
    rows_of = (mine, theirs)
    loads = []
    for side in range(2):
        for n, ref in enumerate((k_hbm, v_hbm)):
            loads.append(pltpu.make_async_copy(ref.at[halves[side]], parcel.at[side, n], load_sem.at[side * 2 + n]))
    own_loads = [
        pltpu.make_async_copy(ref.at[half], even.at[z, OWN, n, mine, :], load_sem.at[4 + n])
        for n, ref in enumerate((k_hbm, v_hbm))
    ]
    q_load = pltpu.make_async_copy(q_hbm.at[0], q_ref, load_sem.at[6])
    for one in loads + own_loads + [q_load]:
        one.start()

    barrier = pltpu.get_barrier_semaphore()
    partners = (along(-1), along(1), along(-2), along(2), swap_to, across_to, up_to, down_to, opposite_from, core_to)
    for partner in partners:
        pl.semaphore_signal(barrier, inc=1, device_id=partner, device_id_type=MESH)

    start = seq * SHARD
    lane = lax.broadcasted_iota(jnp.int32, (1, 128), 1)
    place = jnp.where(lane < PIECE, lane, lane + (SHARD // 2 - PIECE))
    peak[...] = jnp.full_like(peak, HIDDEN)
    total[...] = jnp.zeros_like(total)
    acc[...] = jnp.zeros_like(acc)
    pos = start + lax.broadcasted_iota(jnp.int32, (SHARD, 128), 0)
    doc_first = jnp.zeros((SHARD, 128), jnp.int32)
    begin = jnp.int32(0)
    for d in range(doc_ref.shape[0]):
        doc_first = jnp.where(pos >= begin, begin, doc_first)
        begin = begin + doc_ref[d]
    first[...] = doc_first - place

    for one in loads:
        one.wait()
    pl.semaphore_wait(barrier, len(partners))

    slice_of = [lax.rem(z + off + 8, 8) for off in OFFSETS]
    started = []

    def copy(src, dst, sems, index, to):
        return pltpu.make_async_remote_copy(
            src_ref=src, dst_ref=dst, send_sem=sems.at[(0,) + index], recv_sem=sems.at[(1,) + index],
            device_id=to, device_id_type=MESH,
        )

    def send(copies):
        for one in copies:
            one.start()
            started.append(one)

    def swap(rows):
        return copy(parcel.at[1], even.at[z, OWN, :, rows, :], piece_sem, (1, 0), swap_to)

    def side_ref(u, side, slot=OWN):
        return even.at[slice_of[u], slot, :, rows_of[side], :]

    def side_source(side):
        return parcel.at[0] if side == 0 else side_ref(0, 1)

    def pieces_out(side):
        out = [
            copy(side_source(side), side_ref(0, side, slot), start_sem, (side, slot), to)
            for slot, to in ((ACROSS, across_to), (OPPOSITE, opposite_to))
        ]
        for u in (1, 2, 3, 4):
            out.append(copy(side_source(side), side_ref(0, side), piece_sem, (side, u), along(-OFFSETS[u])))
        return out

    def piece_in(u, side):
        return copy(side_source(side), side_ref(u, side), piece_sem, (side, u), along(OFFSETS[u]))

    def start_in(slot, side):
        return copy(side_source(side), side_ref(0, side, slot), start_sem, (side, slot), across_to)

    def spread(u, unit):
        ref = even.at[slice_of[unit], OPPOSITE]
        return copy(ref, ref, opposite_sem, (u - 1,), along(-OFFSETS[u]))

    def relay(slot, n, unit, off):
        ref = even.at[slice_of[unit], slot]
        if n >= 2:
            ref = ref.at[n - 2]
        return copy(ref, ref, relay_sem, (slot, n), along(off))

    def relays_out(slot, unit):
        if OFFSETS[unit] == -2:
            return [relay(slot, 0, unit, 1), relay(slot, 2, unit, 2)]
        if OFFSETS[unit] == 2:
            return [relay(slot, 1, unit, -1), relay(slot, 3, unit, -2)]
        return []

    def relays_in(slot, u):
        for n in {5: (0,), 6: (1,), 7: (2, 3)}[u]:
            relay(slot, n, u, 1).wait_recv()

    def across(u):
        return copy(even.at[slice_of[u], OWN], even.at[slice_of[u], ACROSS], across_sem, (u - 1,), across_to)

    up_slot = jnp.where(y == 3, ACROSS, OWN)
    down_slot = jnp.where(y == 0, OWN, ACROSS)

    def up(u):
        return copy(even.at[slice_of[u], up_slot], even.at[slice_of[u], BEHIND], behind_sem, (u,), up_to)

    def down(u):
        return copy(even.at[slice_of[u], down_slot], even.at[slice_of[u], AHEAD], ahead_sem, (u,), down_to)

    def to_core(u):
        return copy(even.at[slice_of[u], pl.ds(core, 4)], odd.at[slice_of[u]], core_sem, (u,), core_to)

    def own_arrives(step):
        for u in ROUNDS[step]:
            if u == 0:
                swap(theirs).wait_recv()
                send(pieces_out(1))
            elif u < 5:
                for side in range(2):
                    piece_in(u, side).wait_recv()
                send(relays_out(OWN, u))
            else:
                relays_in(OWN, u)
            if u:
                send([across(u)])

    def across_arrives(step):
        for u in ROUNDS[step]:
            if u:
                across(u).wait_recv()
            else:
                for side in range(2):
                    start_in(ACROSS, side).wait_recv()
            send([up(u), down(u)])

    def opposite_arrives(step):
        for u in ROUNDS[step]:
            if u == 0:
                for side in range(2):
                    start_in(OPPOSITE, side).wait_recv()
                send([spread(n, 0) for n in (1, 2, 3, 4)])
            elif u < 5:
                spread(u, u).wait_recv()
                send(relays_out(OPPOSITE, u))
            else:
                relays_in(OPPOSITE, u)

    def sides_arrive(step):
        for u in ROUNDS[step]:
            up(u).wait_recv()
            down(u).wait_recv()
            send([to_core(u)])

    def core_arrives(step):
        for u in ROUNDS[step]:
            to_core(u).wait_recv()

    send([swap(mine)])
    send(pieces_out(0))
    for one in own_loads + [q_load]:
        one.wait()

    def base(slot, u, from_sibling):
        if from_sibling:
            back = jnp.where(core == 1, BACK[slot], BACK[slot + 1])
            owner = chip - back
            shard = owner * 2 + (1 - core)
        else:
            owner = chip - BACK[slot]
            shard = owner * 2 + core
        return jnp.where(owner >= 0, shard * SHARD + slice_of[u] * PIECE, FAR)

    def attend(keys, values, bases, causal, blocks):
        groups = len(bases)

        def score(i):
            return lax.dot_general(q_ref[pl.ds(i * BLOCK, BLOCK), :], keys, NT, preferred_element_type=jnp.float32)

        ahead = score(blocks[0])
        for n, i in enumerate(blocks):
            s = ahead
            ahead = score(blocks[n + 1]) if n + 1 < len(blocks) else None
            r = pl.ds(i * BLOCK, BLOCK)
            f = first[r, :]
            if causal:
                line = start + i * BLOCK + lax.broadcasted_iota(jnp.int32, (BLOCK, 128), 0) - place
            cols = []
            for g in range(groups):
                seen = f <= bases[g]
                if causal:
                    seen = seen & (line >= bases[g])
                cols.append(jnp.where(seen, s[:, g * UNIT:(g + 1) * UNIT], HIDDEN))
            top = tree(jnp.maximum, cols)
            old = peak[r, :]
            new = jnp.maximum(old, jnp.max(top, axis=1, keepdims=True))
            shift = new * LOG_SCALE
            factor = jnp.exp2(old * LOG_SCALE - shift)
            peak[r, :] = new
            weights = [jnp.exp2(c * LOG_SCALE - shift) for c in cols]
            total[r, :] = total[r, :] * factor + tree(jnp.add, weights)
            p = jnp.concatenate([w.astype(jnp.bfloat16) for w in weights], axis=1)
            acc[r, :] = acc[r, :] * factor + lax.dot_general(p, values, NN, preferred_element_type=jnp.float32)

    def attend_own(units):
        keys = jnp.concatenate([even[slice_of[u], OWN, 0] for u in units], axis=0)
        values = jnp.concatenate([even[slice_of[u], OWN, 1] for u in units], axis=0)
        attend(keys, values, [base(OWN, u, False) for u in units], True, (0, 1, 2, 3))

    def attend_others(seen_even, seen_odd, blocks=(0, 1, 2, 3)):
        keys, values, bases = [], [], []
        for ref, slots, steps in ((even, range(1, 5), seen_even), (odd, range(4), seen_odd)):
            for u in [u for step in steps for u in ROUNDS[step]]:
                for slot in slots:
                    keys.append(ref[slice_of[u], slot, 0])
                    values.append(ref[slice_of[u], slot, 1])
                    bases.append(base(slot, u, ref is odd))
        attend(jnp.concatenate(keys, axis=0), jnp.concatenate(values, axis=0), bases, False, blocks)

    own_arrives(0)
    across_arrives(0)
    opposite_arrives(0)
    own_arrives(1)
    own_arrives(2)
    attend_own((0, 1, 2, 3, 4))
    sides_arrive(0)
    across_arrives(1)
    opposite_arrives(1)
    attend_others((0,), ())
    across_arrives(2)
    opposite_arrives(2)
    own_arrives(3)
    own_arrives(4)
    sides_arrive(1)
    core_arrives(0)
    attend_others((1,), (0,), (0, 1))
    sides_arrive(2)
    across_arrives(3)
    attend_others((1,), (0,), (2, 3))
    core_arrives(1)
    across_arrives(4)
    opposite_arrives(3)
    attend_others((2,), (1,), (0, 1))
    opposite_arrives(4)
    sides_arrive(3)
    attend_others((2,), (1,), (2, 3))
    sides_arrive(4)
    attend_own((5, 6, 7))
    core_arrives(2)
    attend_others((3, 4), (2,))
    core_arrives(3)
    core_arrives(4)
    attend_others((), (3, 4))
    o_ref[0] = (acc[...] / jnp.sum(total[...], axis=1, keepdims=True)).astype(o_ref.dtype)
    for one in started:
        one.wait_send()


def tree(join, parts):
    while len(parts) > 1:
        rest = [parts[-1]] if len(parts) % 2 else []
        parts = [join(a, b) for a, b in zip(parts[::2], parts[1::2])] + rest
    return parts[0]


def local(query_heads, key_heads, value_heads, doc_lengths):
    _, rows, width = query_heads.shape
    vmem = pl.BlockSpec(memory_space=pltpu.VMEM)

    hbm = pl.BlockSpec(memory_space=pltpu.HBM)

    def sems(*n):
        return pltpu.SemaphoreType.DMA((2,) + n)

    return pl.pallas_call(
        attention_kernel,
        out_shape=jax.ShapeDtypeStruct(query_heads.shape, jnp.bfloat16),
        in_specs=[pl.BlockSpec(memory_space=pltpu.SMEM), hbm, hbm, hbm],
        out_specs=vmem,
        scratch_shapes=[
            pltpu.VMEM((8, 5, 2, UNIT, width), jnp.bfloat16),
            pltpu.VMEM((8, 4, 2, UNIT, width), jnp.bfloat16),
            pltpu.VMEM((2, 2, PIECE, width), jnp.bfloat16),
            pltpu.VMEM((rows, width), jnp.bfloat16),
            pltpu.VMEM((rows, width), jnp.float32),
            pltpu.VMEM((rows, 128), jnp.float32),
            pltpu.VMEM((rows, 128), jnp.float32),
            pltpu.VMEM((rows, 128), jnp.int32),
            pltpu.SemaphoreType.DMA((7,)),
            sems(2, 5), sems(4), sems(2, 4), sems(2, 5), sems(7), sems(8), sems(8), sems(8),
        ],
        compiler_params=pltpu.CompilerParams(
            collective_id=0, has_side_effects=True, vmem_limit_bytes=48 * 2**20
        ),
        name="attention",
    )(doc_lengths, query_heads, key_heads, value_heads)


def solution(mesh):
    placed = (
        P("head", "seq", None),
        P(None, ("seq", "head"), None),
        P(None, ("seq", "head"), None),
        P(),
    )
    return jax.shard_map(
        local, mesh=mesh, in_specs=placed, out_specs=P("head", "seq", None), check_vma=False
    )
```

time: 51.1 us -> 48 us (0.939)
  the two profiles are of different devices: /device:TPU:8 before, /device:TPU:32 now
where the time goes in v3:
time: 48 us; the launch traced here: 47.7 us
  Pallas kernels  43.9 us (91%)
  local copies, waits for them, and re-layouts  3.82 us (8%)
    pallas_call x1, Pallas kernels, local(): pl.pallas_call(attention_kernel, out_shape=jax.ShapeDtypeStruct(query_hea...  43.9 us
    unnamed x9, local copies, waits for them, and re-layouts  3.82 us

profile of v3, /device:TPU:32, one launch (start us, length us, event | category | flops | bytes accessed | tf_op | source)
XLA Modules:
  0.0 47.7 jit_solution(5159346917891407467)
XLA Ops:
  0.0 0.0 copy-start
  0.0 0.9 %copy-done = bf16[1,1024,128]{2,1,0:T(8,128)(2,1)S(1)} copy-done((bf16[1,1024,128]{2,1,0:T(8,128)(2,1)S(1)}, bf16[1,1024,128]{2,1,0:T(8,128)(2,1)}, u32[]{:S(2)}) %copy-start) | copy-done | bytes 262168
  1.0 0.0 copy-start.1
  1.0 0.8 %copy-done.1 = bf16[2,64,128]{2,1,0:T(8,128)(2,1)S(1)} copy-done((bf16[2,64,128]{2,1,0:T(8,128)(2,1)S(1)}, bf16[2,64,128]{2,1,0:T(8,128)(2,1)}, u32[]{:S(2)}) %copy-start.1) | copy-done | bytes 32792
  1.7 0.0 copy-start.2
  1.7 0.8 %copy-done.2 = bf16[2,64,128]{2,1,0:T(8,128)(2,1)S(1)} copy-done((bf16[2,64,128]{2,1,0:T(8,128)(2,1)S(1)}, bf16[2,64,128]{2,1,0:T(8,128)(2,1)}, u32[]{:S(2)}) %copy-start.2) | copy-done | bytes 32792
  2.5 0.0 copy-start.3
  2.5 0.7 %copy-done.3 = s32[16]{0:T(128)S(1)} copy-done((s32[16]{0:T(128)S(1)}, s32[16]{0:T(128)}, u32[]{:S(2)}) %copy-start.3) | copy-done | bytes 88
  3.1 43.9 %attention.1 = bf16[1,1024,128]{2,1,0:T(8,128)(2,1)S(1)} custom-call(s32[16]{0:T(128)S(1)} %copy-done.3, bf16[1,1024,128]{2,1,0:T(8,128)(2,1)S(1)} %copy-done, bf16[2,64,128]{2,1,0:T(8,128)(2,1)S(1)} %copy-done.1, bf16[2,64,128]{2,1,0:T(8,128)(2,1)S(1)} %copy-done.2), custom_call_target="tpu_custom_call" | custom-call | tf_op jit(solution)/shard_map/attention/pallas_call | solution.py:325
  47.0 0.7 %copy.6 = bf16[1,1024,128]{2,1,0:T(8,128)(2,1)} copy(bf16[1,1024,128]{2,1,0:T(8,128)(2,1)S(1)} %attention.1) | data formatting | bytes 524288
Async XLA Ops:
  0.0 0.9 %copy-start = (bf16[1,1024,128]{2,1,0:T(8,128)(2,1)S(1)}, bf16[1,1024,128]{2,1,0:T(8,128)(2,1)}, u32[]{:S(2)}) copy-start(bf16[1,1024,128]{2,1,0:T(8,128)(2,1)} %q_hbm.1) | copy-start | bytes 786436
  1.0 0.8 %copy-start.1 = (bf16[2,64,128]{2,1,0:T(8,128)(2,1)S(1)}, bf16[2,64,128]{2,1,0:T(8,128)(2,1)}, u32[]{:S(2)}) copy-start(bf16[2,64,128]{2,1,0:T(8,128)(2,1)} %k_hbm.1) | copy-start | bytes 98308
  1.7 0.8 %copy-start.2 = (bf16[2,64,128]{2,1,0:T(8,128)(2,1)S(1)}, bf16[2,64,128]{2,1,0:T(8,128)(2,1)}, u32[]{:S(2)}) copy-start(bf16[2,64,128]{2,1,0:T(8,128)(2,1)} %v_hbm.1) | copy-start | bytes 98308
  2.5 0.7 %copy-start.3 = (s32[16]{0:T(128)S(1)}, s32[16]{0:T(128)}, u32[]{:S(2)}) copy-start(s32[16]{0:T(128)} %doc_ref.1) | copy-start | bytes 196

commit v4 on v3

--- a/solution.py
+++ b/solution.py
@@ -21,12 +21,11 @@
 OWN, OPPOSITE, BEHIND, AHEAD, ACROSS = range(5)
 BACK = (0, 2, 1, 3, 4)
 OFFSETS = (0, -1, 1, -2, 2, -3, 3, -4)
-ROUNDS = ((0,), (1, 2), (3, 4), (5, 6), (7,))
 
 
 def attention_kernel(
     doc_ref, q_hbm, k_hbm, v_hbm, o_ref,
-    even, odd, parcel, q_ref, acc, peak, total, first,
+    even, odd, parcel, q_ref, acc, peak, first,
     load_sem, piece_sem, opposite_sem, relay_sem, start_sem, across_sem, behind_sem, ahead_sem, core_sem,
 ):
     seq, head = lax.axis_index("seq"), lax.axis_index("head")
@@ -73,7 +72,6 @@
     lane = lax.broadcasted_iota(jnp.int32, (1, 128), 1)
     place = jnp.where(lane < PIECE, lane, lane + (SHARD // 2 - PIECE))
     peak[...] = jnp.full_like(peak, HIDDEN)
-    total[...] = jnp.zeros_like(total)
     acc[...] = jnp.zeros_like(acc)
     pos = start + lax.broadcasted_iota(jnp.int32, (SHARD, 128), 0)
     doc_first = jnp.zeros((SHARD, 128), jnp.int32)
@@ -161,8 +159,8 @@
     def to_core(u):
         return copy(even.at[slice_of[u], pl.ds(core, 4)], odd.at[slice_of[u]], core_sem, (u,), core_to)
 
-    def own_arrives(step):
-        for u in ROUNDS[step]:
+    def own_arrives(*units):
+        for u in units:
             if u == 0:
                 swap(theirs).wait_recv()
                 send(pieces_out(1))
@@ -175,8 +173,8 @@
             if u:
                 send([across(u)])
 
-    def across_arrives(step):
-        for u in ROUNDS[step]:
+    def across_arrives(*units):
+        for u in units:
             if u:
                 across(u).wait_recv()
             else:
@@ -184,8 +182,8 @@
                     start_in(ACROSS, side).wait_recv()
             send([up(u), down(u)])
 
-    def opposite_arrives(step):
-        for u in ROUNDS[step]:
+    def opposite_arrives(*units):
+        for u in units:
             if u == 0:
                 for side in range(2):
                     start_in(OPPOSITE, side).wait_recv()
@@ -196,14 +194,14 @@
             else:
                 relays_in(OPPOSITE, u)
 
-    def sides_arrive(step):
-        for u in ROUNDS[step]:
+    def sides_arrive(*units):
+        for u in units:
             up(u).wait_recv()
             down(u).wait_recv()
             send([to_core(u)])
 
-    def core_arrives(step):
-        for u in ROUNDS[step]:
+    def core_arrives(*units):
+        for u in units:
             to_core(u).wait_recv()
 
     send([swap(mine)])
@@ -223,6 +221,7 @@
 
     def attend(keys, values, bases, causal, blocks):
         groups = len(bases)
+        values = jnp.concatenate([values, jnp.ones_like(values)], axis=1)
 
         def score(i):
             return lax.dot_general(q_ref[pl.ds(i * BLOCK, BLOCK), :], keys, NT, preferred_element_type=jnp.float32)
@@ -248,19 +247,26 @@
             factor = jnp.exp2(old * LOG_SCALE - shift)
             peak[r, :] = new
             weights = [jnp.exp2(c * LOG_SCALE - shift) for c in cols]
-            total[r, :] = total[r, :] * factor + tree(jnp.add, weights)
             p = jnp.concatenate([w.astype(jnp.bfloat16) for w in weights], axis=1)
-            acc[r, :] = acc[r, :] * factor + lax.dot_general(p, values, NN, preferred_element_type=jnp.float32)
+            product = lax.dot_general(p, values, NN, preferred_element_type=jnp.float32)
+            for part in (pl.ds(0, 128), pl.ds(128, 128)):
+                acc[r, part] = acc[r, part] * factor + product[:, part.start:part.start + 128]
 
     def attend_own(units):
-        keys = jnp.concatenate([even[slice_of[u], OWN, 0] for u in units], axis=0)
-        values = jnp.concatenate([even[slice_of[u], OWN, 1] for u in units], axis=0)
-        attend(keys, values, [base(OWN, u, False) for u in units], True, (0, 1, 2, 3))
+        keys, values = [[even[slice_of[u], OWN, n, pl.ds(0, PIECE)] for u in units] for n in range(2)]
+        bases = [
+            jnp.where(lane < PIECE, base(OWN, a, False), base(OWN, b, False) - SHARD // 2)
+            for a, b in zip(units[::2], units[1::2])
+        ]
+        attend(jnp.concatenate(keys, axis=0), jnp.concatenate(values, axis=0), bases, True, (0, 1))
+        keys, values = [[even[slice_of[u], OWN, n] for u in units] for n in range(2)]
+        bases = [base(OWN, u, False) for u in units]
+        attend(jnp.concatenate(keys, axis=0), jnp.concatenate(values, axis=0), bases, True, (2, 3))
 
     def attend_others(seen_even, seen_odd, blocks=(0, 1, 2, 3)):
         keys, values, bases = [], [], []
-        for ref, slots, steps in ((even, range(1, 5), seen_even), (odd, range(4), seen_odd)):
-            for u in [u for step in steps for u in ROUNDS[step]]:
+        for ref, slots, units in ((even, range(1, 5), seen_even), (odd, range(4), seen_odd)):
+            for u in units:
                 for slot in slots:
                     keys.append(ref[slice_of[u], slot, 0])
                     values.append(ref[slice_of[u], slot, 1])
@@ -268,40 +274,47 @@
         attend(jnp.concatenate(keys, axis=0), jnp.concatenate(values, axis=0), bases, False, blocks)
 
     own_arrives(0)
+    own_arrives(1)
+    own_arrives(2)
+    own_arrives(3)
+    own_arrives(4)
     across_arrives(0)
     opposite_arrives(0)
-    own_arrives(1)
-    own_arrives(2)
-    attend_own((0, 1, 2, 3, 4))
+    attend_own((0, 1, 2, 3))
+    across_arrives(1)
+    across_arrives(2)
+    own_arrives(5)
+    own_arrives(6)
+    own_arrives(7)
     sides_arrive(0)
-    across_arrives(1)
-    opposite_arrives(1)
     attend_others((0,), ())
-    across_arrives(2)
-    opposite_arrives(2)
-    own_arrives(3)
-    own_arrives(4)
+    across_arrives(3)
+    across_arrives(4)
+    opposite_arrives(1, 2)
+    opposite_arrives(3, 4)
+    attend_own((4, 5, 6, 7))
     sides_arrive(1)
+    sides_arrive(2)
     core_arrives(0)
-    attend_others((1,), (0,), (0, 1))
-    sides_arrive(2)
-    across_arrives(3)
-    attend_others((1,), (0,), (2, 3))
-    core_arrives(1)
-    across_arrives(4)
-    opposite_arrives(3)
-    attend_others((2,), (1,), (0, 1))
-    opposite_arrives(4)
+    attend_others((1, 2), (0,), (0, 1))
+    across_arrives(5)
+    across_arrives(6)
+    across_arrives(7)
+    attend_others((1, 2), (0,), (2, 3))
     sides_arrive(3)
-    attend_others((2,), (1,), (2, 3))
     sides_arrive(4)
-    attend_own((5, 6, 7))
-    core_arrives(2)
-    attend_others((3, 4), (2,))
-    core_arrives(3)
-    core_arrives(4)
-    attend_others((), (3, 4))
-    o_ref[0] = (acc[...] / jnp.sum(total[...], axis=1, keepdims=True)).astype(o_ref.dtype)
+    opposite_arrives(5, 6, 7)
+    core_arrives(1, 2)
+    attend_others((3, 4), (1, 2), (0, 1))
+    sides_arrive(5)
+    sides_arrive(6)
+    sides_arrive(7)
+    attend_others((3, 4), (1, 2), (2, 3))
+    core_arrives(3, 4)
+    attend_others((5, 6, 7), (3, 4))
+    core_arrives(5, 6, 7)
+    attend_others((), (5, 6, 7))
+    o_ref[0] = (acc[:, :128] / acc[:, 128:]).astype(o_ref.dtype)
     for one in started:
         one.wait_send()
 
@@ -332,8 +345,7 @@
             pltpu.VMEM((8, 4, 2, UNIT, width), jnp.bfloat16),
             pltpu.VMEM((2, 2, PIECE, width), jnp.bfloat16),
             pltpu.VMEM((rows, width), jnp.bfloat16),
-            pltpu.VMEM((rows, width), jnp.float32),
-            pltpu.VMEM((rows, 128), jnp.float32),
+            pltpu.VMEM((rows, 2 * width), jnp.float32),
             pltpu.VMEM((rows, 128), jnp.float32),
             pltpu.VMEM((rows, 128), jnp.int32),
             pltpu.SemaphoreType.DMA((7,)),

time: 48 us -> 45.2 us (0.942)
  the two profiles are of different devices: /device:TPU:32 before, /device:TPU:8 now
where the time goes in v4:
time: 45.2 us; the launch traced here: 44.9 us
  Pallas kernels  41.1 us (91%)
  local copies, waits for them, and re-layouts  3.82 us (8%)
    pallas_call x1, Pallas kernels, local(): pl.pallas_call(attention_kernel, out_shape=jax.ShapeDtypeStruct(query_hea...  41.1 us
    unnamed x9, local copies, waits for them, and re-layouts  3.82 us

profile of v4, /device:TPU:8, one launch (start us, length us, event | category | flops | bytes accessed | tf_op | source)
XLA Modules:
  0.0 44.9 jit_solution(17666807263036518976)
XLA Ops:
  0.0 0.0 copy-start
  0.0 0.9 %copy-done = bf16[1,1024,128]{2,1,0:T(8,128)(2,1)S(1)} copy-done((bf16[1,1024,128]{2,1,0:T(8,128)(2,1)S(1)}, bf16[1,1024,128]{2,1,0:T(8,128)(2,1)}, u32[]{:S(2)}) %copy-start) | copy-done | bytes 262168
  1.0 0.0 copy-start.1
  1.0 0.8 %copy-done.1 = bf16[2,64,128]{2,1,0:T(8,128)(2,1)S(1)} copy-done((bf16[2,64,128]{2,1,0:T(8,128)(2,1)S(1)}, bf16[2,64,128]{2,1,0:T(8,128)(2,1)}, u32[]{:S(2)}) %copy-start.1) | copy-done | bytes 32792
  1.7 0.0 copy-start.2
  1.7 0.8 %copy-done.2 = bf16[2,64,128]{2,1,0:T(8,128)(2,1)S(1)} copy-done((bf16[2,64,128]{2,1,0:T(8,128)(2,1)S(1)}, bf16[2,64,128]{2,1,0:T(8,128)(2,1)}, u32[]{:S(2)}) %copy-start.2) | copy-done | bytes 32792
  2.5 0.0 copy-start.3
  2.5 0.7 %copy-done.3 = s32[16]{0:T(128)S(1)} copy-done((s32[16]{0:T(128)S(1)}, s32[16]{0:T(128)}, u32[]{:S(2)}) %copy-start.3) | copy-done | bytes 88
  3.1 41.1 %attention.1 = bf16[1,1024,128]{2,1,0:T(8,128)(2,1)S(1)} custom-call(s32[16]{0:T(128)S(1)} %copy-done.3, bf16[1,1024,128]{2,1,0:T(8,128)(2,1)S(1)} %copy-done, bf16[2,64,128]{2,1,0:T(8,128)(2,1)S(1)} %copy-done.1, bf16[2,64,128]{2,1,0:T(8,128)(2,1)S(1)} %copy-done.2), custom_call_target="tpu_custom_call" | custom-call | tf_op jit(solution)/shard_map/attention/pallas_call | solution.py:338
  44.2 0.7 %copy.6 = bf16[1,1024,128]{2,1,0:T(8,128)(2,1)} copy(bf16[1,1024,128]{2,1,0:T(8,128)(2,1)S(1)} %attention.1) | data formatting | bytes 524288
Async XLA Ops:
  0.0 0.9 %copy-start = (bf16[1,1024,128]{2,1,0:T(8,128)(2,1)S(1)}, bf16[1,1024,128]{2,1,0:T(8,128)(2,1)}, u32[]{:S(2)}) copy-start(bf16[1,1024,128]{2,1,0:T(8,128)(2,1)} %q_hbm.1) | copy-start | bytes 786436
  1.0 0.8 %copy-start.1 = (bf16[2,64,128]{2,1,0:T(8,128)(2,1)S(1)}, bf16[2,64,128]{2,1,0:T(8,128)(2,1)}, u32[]{:S(2)}) copy-start(bf16[2,64,128]{2,1,0:T(8,128)(2,1)} %k_hbm.1) | copy-start | bytes 98308
  1.7 0.8 %copy-start.2 = (bf16[2,64,128]{2,1,0:T(8,128)(2,1)S(1)}, bf16[2,64,128]{2,1,0:T(8,128)(2,1)}, u32[]{:S(2)}) copy-start(bf16[2,64,128]{2,1,0:T(8,128)(2,1)} %v_hbm.1) | copy-start | bytes 98308
  2.5 0.7 %copy-start.3 = (s32[16]{0:T(128)S(1)}, s32[16]{0:T(128)}, u32[]{:S(2)}) copy-start(s32[16]{0:T(128)} %doc_ref.1) | copy-start | bytes 196

commit v5 on v4

--- a/solution.py
+++ b/solution.py
@@ -219,21 +219,21 @@
             shard = owner * 2 + core
         return jnp.where(owner >= 0, shard * SHARD + slice_of[u] * PIECE, FAR)
 
-    def attend(keys, values, bases, causal, blocks):
+    def attend(keys, values, bases, causal, blocks, block=BLOCK):
         groups = len(bases)
         values = jnp.concatenate([values, jnp.ones_like(values)], axis=1)
 
         def score(i):
-            return lax.dot_general(q_ref[pl.ds(i * BLOCK, BLOCK), :], keys, NT, preferred_element_type=jnp.float32)
+            return lax.dot_general(q_ref[pl.ds(i * block, block), :], keys, NT, preferred_element_type=jnp.float32)
 
         ahead = score(blocks[0])
         for n, i in enumerate(blocks):
             s = ahead
             ahead = score(blocks[n + 1]) if n + 1 < len(blocks) else None
-            r = pl.ds(i * BLOCK, BLOCK)
+            r = pl.ds(i * block, block)
             f = first[r, :]
             if causal:
-                line = start + i * BLOCK + lax.broadcasted_iota(jnp.int32, (BLOCK, 128), 0) - place
+                line = start + i * block + lax.broadcasted_iota(jnp.int32, (block, 128), 0) - place
             cols = []
             for g in range(groups):
                 seen = f <= bases[g]
@@ -263,7 +263,7 @@
         bases = [base(OWN, u, False) for u in units]
         attend(jnp.concatenate(keys, axis=0), jnp.concatenate(values, axis=0), bases, True, (2, 3))
 
-    def attend_others(seen_even, seen_odd, blocks=(0, 1, 2, 3)):
+    def attend_others(seen_even, seen_odd, blocks=(0, 1, 2, 3), block=BLOCK):
         keys, values, bases = [], [], []
         for ref, slots, units in ((even, range(1, 5), seen_even), (odd, range(4), seen_odd)):
             for u in units:
@@ -271,7 +271,7 @@
                     keys.append(ref[slice_of[u], slot, 0])
                     values.append(ref[slice_of[u], slot, 1])
                     bases.append(base(slot, u, ref is odd))
-        attend(jnp.concatenate(keys, axis=0), jnp.concatenate(values, axis=0), bases, False, blocks)
+        attend(jnp.concatenate(keys, axis=0), jnp.concatenate(values, axis=0), bases, False, blocks, block)
 
     own_arrives(0)
     own_arrives(1)
@@ -311,9 +311,9 @@
     sides_arrive(7)
     attend_others((3, 4), (1, 2), (2, 3))
     core_arrives(3, 4)
-    attend_others((5, 6, 7), (3, 4))
+    attend_others((5, 6, 7), (3, 4), (0, 1), 2 * BLOCK)
     core_arrives(5, 6, 7)
-    attend_others((), (5, 6, 7))
+    attend_others((), (5, 6, 7), (0, 1), 2 * BLOCK)
     o_ref[0] = (acc[:, :128] / acc[:, 128:]).astype(o_ref.dtype)
     for one in started:
         one.wait_send()
@@ -352,7 +352,7 @@
             sems(2, 5), sems(4), sems(2, 4), sems(2, 5), sems(7), sems(8), sems(8), sems(8),
         ],
         compiler_params=pltpu.CompilerParams(
-            collective_id=0, has_side_effects=True, vmem_limit_bytes=48 * 2**20
+            collective_id=0, has_side_effects=True, vmem_limit_bytes=65000 * 2**10
         ),
         name="attention",
     )(doc_lengths, query_heads, key_heads, value_heads)

time: 45.2 us -> 43.3 us (0.958)
  local copies, waits for them, and re-layouts: 3.82 us -> 1.67 us
    unnamed x9 -> x1, local copies, waits for them, and re-layouts: 3.82 us -> 1.67 us
where the time goes in v5:
time: 43.3 us; the launch traced here: 43.2 us
  Pallas kernels  41.5 us (96%)
  local copies, waits for them, and re-layouts  1.67 us (4%)
    pallas_call x1, Pallas kernels, local(): pl.pallas_call(attention_kernel, out_shape=jax.ShapeDtypeStruct(query_hea...  41.5 us
    unnamed x1, local copies, waits for them, and re-layouts  1.67 us

profile of v5, /device:TPU:8, one launch (start us, length us, event | category | flops | bytes accessed | tf_op | source)
XLA Modules:
  0.0 43.2 jit_solution(5105834513567851943)
XLA Ops:
  0.0 41.5 %attention.1 = bf16[1,1024,128]{2,1,0:T(8,128)(2,1)} custom-call(s32[16]{0:T(128)} %doc_ref.1, bf16[1,1024,128]{2,1,0:T(8,128)(2,1)} %q_hbm.1, bf16[2,64,128]{2,1,0:T(8,128)(2,1)} %k_hbm.1, bf16[2,64,128]{2,1,0:T(8,128)(2,1)} %v_hbm.1), custom_call_target="tpu_custom_call" | custom-call | tf_op jit(solution)/shard_map/attention/pallas_call | solution.py:338
  41.5 1.7 %copy.6 = bf16[1,1024,128]{2,1,0:T(8,128)(2,1)} copy(bf16[1,1024,128]{2,1,0:T(8,128)(2,1)} %attention.1) | data formatting | bytes 524288

commit v6 on v5

--- a/solution.py
+++ b/solution.py
@@ -47,6 +47,11 @@
     up_to = at(x * 4 + lax.rem(y + 1, 4), core, half, z)
     down_to = at(x * 4 + lax.rem(y + 3, 4), core, half, z)
     core_to = at(chip, 1 - core, half, z)
+
+    barrier = pltpu.get_barrier_semaphore()
+    partners = (along(-1), along(1), along(-2), along(2), swap_to, across_to, up_to, down_to, opposite_from, core_to)
+    for partner in partners:
+        pl.semaphore_signal(barrier, inc=1, device_id=partner, device_id_type=MESH)
 
     mine = pl.ds(pl.multiple_of(half * PIECE, PIECE), PIECE)
     theirs = pl.ds(pl.multiple_of((1 - half) * PIECE, PIECE), PIECE)
@@ -62,11 +67,6 @@
     q_load = pltpu.make_async_copy(q_hbm.at[0], q_ref, load_sem.at[6])
     for one in loads + own_loads + [q_load]:
         one.start()
-
-    barrier = pltpu.get_barrier_semaphore()
-    partners = (along(-1), along(1), along(-2), along(2), swap_to, across_to, up_to, down_to, opposite_from, core_to)
-    for partner in partners:
-        pl.semaphore_signal(barrier, inc=1, device_id=partner, device_id_type=MESH)
 
     start = seq * SHARD
     lane = lax.broadcasted_iota(jnp.int32, (1, 128), 1)
@@ -296,9 +296,9 @@
     sides_arrive(1)
     sides_arrive(2)
     core_arrives(0)
-    attend_others((1, 2), (0,), (0, 1))
     across_arrives(5)
     across_arrives(6)
+    attend_others((1, 2), (0,), (0, 1))
     across_arrives(7)
     attend_others((1, 2), (0,), (2, 3))
     sides_arrive(3)

time: 43.3 us -> 42.5 us (0.982)
  Pallas kernels: 41.5 us -> 40.4 us
    pallas_call x1, Pallas kernels: 41.5 us -> 40.4 us  [local(): pl.pallas_call(attention_kernel, out_shape=jax.ShapeDtypeStruct(query_hea...]
where the time goes in v6:
time: 42.5 us; the launch traced here: 42.1 us
  Pallas kernels  40.4 us (95%)
  local copies, waits for them, and re-layouts  1.67 us (4%)
    pallas_call x1, Pallas kernels, local(): pl.pallas_call(attention_kernel, out_shape=jax.ShapeDtypeStruct(query_hea...  40.4 us
    unnamed x1, local copies, waits for them, and re-layouts  1.67 us

profile of v6, /device:TPU:8, one launch (start us, length us, event | category | flops | bytes accessed | tf_op | source)
XLA Modules:
  0.0 42.1 jit_solution(12730951406716179107)
XLA Ops:
  0.0 40.4 %attention.1 = bf16[1,1024,128]{2,1,0:T(8,128)(2,1)} custom-call(s32[16]{0:T(128)} %doc_ref.1, bf16[1,1024,128]{2,1,0:T(8,128)(2,1)} %q_hbm.1, bf16[2,64,128]{2,1,0:T(8,128)(2,1)} %k_hbm.1, bf16[2,64,128]{2,1,0:T(8,128)(2,1)} %v_hbm.1), custom_call_target="tpu_custom_call" | custom-call | tf_op jit(solution)/shard_map/attention/pallas_call | solution.py:338
  40.4 1.7 %copy.6 = bf16[1,1024,128]{2,1,0:T(8,128)(2,1)} copy(bf16[1,1024,128]{2,1,0:T(8,128)(2,1)} %attention.1) | data formatting | bytes 524288
